TPU v7x, 32 devices: a whole 2x2x4 slice. The times are simulated.
32 devices in a mesh: lon: 16 (over z, y, core), lat: 2 (over x).
Axes of the slice: x: 2, y: 2, z: 4, core: 2. Of those that a mesh axis runs over, the one named last changes fastest.
Arguments:
- thermal_deviation: float32 [8, 128, 2048], P(None, 'lat', 'lon'), may hold values from -6 to 6
- saltiness_deviation: float32 [8, 128, 2048], P(None, 'lat', 'lon'), may hold values from -6 to 6
- zonal_current_speed: float32 [8, 128, 2048], P(None, 'lat', 'lon'), may hold values from -3 to 3
- meridional_flow_speed: float32 [8, 128, 2048], P(None, 'lat', 'lon'), may hold values from -3 to 3
- water_indicator: int32 [8, 128, 2048], P(None, 'lat', 'lon'), may hold values 0 or 1
Outputs:
- new_temperature: float32 [8, 128, 2048], P(None, 'lat', 'lon')
- new_salinity: float32 [8, 128, 2048], P(None, 'lat', 'lon')
- new_zonal: float32 [8, 128, 2048], P(None, 'lat', 'lon')
- new_meridional: float32 [8, 128, 2048], P(None, 'lat', 'lon')
All inputs are finite; a program needn't handle non-finite values. No bound on the sum of `water_indicator` on one device may be relied on, other than what follows from the above.
Results may differ from a plain program's by a relative error of at most 0.00002.
Values sent between devices are 32-bit elements; how exact they have to be, the bound alone decides.
A program may use at most 64 MiB of HBM per device.

v0:
```python
import functools

import jax
import jax.numpy as jnp
from jax import lax
from jax.experimental import pallas as pl
from jax.experimental.pallas import tpu as pltpu
from jax.sharding import PartitionSpec as P

STEPS = 4
HALO = 8

DIFFUSION = 0.1
HYPERDIFF = 0.01
ADVECTION = 0.25
EXPANSION = 0.2
CONTRACTION = 0.15
PRESSURE_COEF = 0.05
CORIOLIS_MAX = 0.3

MESH = pl.DeviceIdType.MESH
LANES = 128
SUB = 8


def lane_of(shape):
    return lax.broadcasted_iota(jnp.int32, shape, len(shape) - 1)


def take(x, idx):
    return jnp.take_along_axis(x, idx, axis=1)


def swap_bits(regs, lane):
    regs = list(regs)
    for k in range(3):
        dist = 16 << k
        low = (lane & dist) == 0
        for a in range(8):
            if a & (1 << k):
                continue
            b = a | (1 << k)
            x, y = regs[a], regs[b]
            regs[a] = jnp.where(low, x, pltpu.roll(y, dist, 1))
            regs[b] = jnp.where(low, pltpu.roll(x, LANES - dist, 1), y)
    return regs


def kernel(n_lon, n_lat, rows, t_in, s_in, u_in, v_in, m_in, t_out, s_out, u_out, v_out,
           raw, g, pm, lm, part, tot, coef, ax, ay, weak, cor,
           fold, send_w, send_e, recv_w, recv_e, ssem, rsem):
    lo = 2 * SUB
    hi = lo + rows
    blocks = rows // SUB
    half = rows // 2
    lon = lax.axis_index("lon")
    lat = lax.axis_index("lat")
    east = lax.rem(lon + 1, n_lon)
    west = lax.rem(lon + n_lon - 1, n_lon)
    mirror = n_lon - 1 - lon
    is_north = lat == n_lat - 1
    has_south = lat > 0
    north_lat = jnp.where(is_north, lat, lat + 1)
    north_lon = jnp.where(is_north, mirror, lon)
    ins = (t_in, s_in, u_in, v_in, m_in)
    outs = (t_out, s_out, u_out, v_out)

    barrier = pltpu.get_barrier_semaphore()
    for target in ((west, lat), (east, lat), (north_lon, north_lat)):
        pl.semaphore_signal(barrier, inc=1, device_id=target, device_id_type=MESH)

    @pl.when(has_south)
    def _():
        pl.semaphore_signal(barrier, inc=1, device_id=(lon, lat - 1), device_id_type=MESH)

    lane = lane_of((SUB, LANES))
    to_flat = 16 * (lane & 7) + (lane >> 3)
    to_cols = 8 * (lane & 15) + (lane >> 4)
    turned = 8 * (15 - (lane >> 3)) + (lane & 7)
    row8 = lax.broadcasted_iota(jnp.int32, (SUB, LANES), 0)

    def bring(b):
        r = pl.multiple_of(b * SUB, SUB)
        for a in range(5):
            regs = [ins[a][l, pl.ds(r, SUB), :] for l in range(8)]
            if a == 4:
                regs = [x.astype(jnp.float32) for x in regs]
            regs = swap_bits(regs, lane)
            for c in range(8):
                raw[a, c, pl.ds(lo + r, SUB), :] = take(regs[c], to_flat)

    def reverse_rows(x):
        for k in (4, 2, 1):
            up = pltpu.roll(x, SUB - k, 0)
            if k == 4:
                x = up
            else:
                x = jnp.where((row8 & k) == 0, up, pltpu.roll(x, k, 0))
        return x

    def fold_chunk(target, source):
        for a in range(5):
            x = raw[a, source, hi - SUB:hi, :]
            x = reverse_rows(take(x, turned))
            if a in (2, 3):
                x = -x
            fold[a, target] = x

    def copy(src, dst, k, target):
        return pltpu.make_async_remote_copy(
            src_ref=src, dst_ref=dst, send_sem=ssem.at[k], recv_sem=rsem.at[k],
            device_id=target, device_id_type=MESH)

    main = slice(0, 8)
    side = slice(8, 9)

    def to_north(part_slice, k):
        return copy(raw.at[:, part_slice, hi - SUB:hi], raw.at[:, part_slice, lo - SUB:lo],
                    k, (lon, lat + 1))

    def to_fold(part_slice, k):
        return copy(fold.at[:, part_slice], raw.at[:, part_slice, hi:hi + SUB],
                    k, (mirror, lat))

    def to_south(part_slice, k):
        return copy(raw.at[:, part_slice, lo:lo + SUB], raw.at[:, part_slice, hi:hi + SUB],
                    k, (lon, lat - 1))

    bring(blocks - 1)
    bring(0)

    @pl.when(is_north)
    def _():
        for c in range(8):
            fold_chunk(c, 7 - c)

    pl.semaphore_wait(barrier, jnp.where(has_south, 4, 3))

    def send_main():
        @pl.when(is_north)
        def _():
            to_fold(main, 0).start()

        @pl.when(jnp.logical_not(is_north))
        def _():
            to_north(main, 1).start()

        @pl.when(has_south)
        def _():
            to_south(main, 2).start()

    def send_side():
        @pl.when(is_north)
        def _():
            to_fold(side, 3).start()

        @pl.when(jnp.logical_not(is_north))
        def _():
            to_north(side, 4).start()

        @pl.when(has_south)
        def _():
            to_south(side, 5).start()

    send_main()

    @pl.loop(1, blocks - 1)
    def _(b):
        bring(b)

    near = lane_of((half, LANES)) < 64
    for a in range(5):
        first = raw[a, 0, lo:lo + half]
        second = raw[a, 0, lo + half:hi]
        send_w[a] = jnp.where(near, first, pltpu.roll(second, 64, 1))
        first = raw[a, 7, lo:lo + half]
        second = raw[a, 7, lo + half:hi]
        send_e[a] = jnp.where(near, pltpu.roll(first, 64, 1), second)
    go_w = copy(send_w, recv_e, 6, (west, lat))
    go_e = copy(send_e, recv_w, 7, (east, lat))
    go_w.start()
    go_e.start()

    nothing = jnp.zeros((9, SUB, LANES), jnp.float32)
    for ref in (raw, g, lm):
        for a in range(ref.shape[0]):
            ref[a, :, 0:SUB, :] = nothing
            ref[a, :, hi + SUB:hi + 2 * SUB, :] = nothing
    for r in (0, hi + SUB):
        pm[:, r:r + SUB, :] = nothing

    @pl.when(jnp.logical_not(has_south))
    def _():
        for a in range(5):
            raw[a, :, lo - SUB:lo, :] = nothing

    go_w.wait()
    go_e.wait()
    for a in range(5):
        x, y = recv_e[a], recv_w[a]
        raw[a, 8, lo:lo + half] = jnp.where(near, x, pltpu.roll(y, 64, 1))
        raw[a, 8, lo + half:hi] = jnp.where(near, pltpu.roll(x, 64, 1), y)

    @pl.when(is_north)
    def _():
        fold_chunk(8, 8)

    send_side()

    level = lane & 7
    scale = 0.5 * PRESSURE_COEF
    total = rows * n_lat

    def pressure(temperature, salinity):
        p = (scale * CONTRACTION) * salinity - (scale * EXPANSION) * temperature
        for k in (1, 2, 4):
            p = p + jnp.where(level >= k, pltpu.roll(p, k, 1), 0.0)
        return p

    def block(b):
        return pl.ds(pl.multiple_of(b * SUB, SUB), SUB)

    def columns(ref, lead, c, at):
        x = ref[(*lead, c, at, slice(None))]
        xe = ref[(*lead, (c + 1) % 9, at, slice(None))]
        xw = ref[(*lead, (c + 8) % 9, at, slice(None))]
        return (pltpu.roll(jnp.where(lane < 8, xe, x), LANES - 8, 1),
                pltpu.roll(jnp.where(lane >= LANES - 8, xw, x), 8, 1))

    def lines(ref, lead, c, b):
        return (ref[(*lead, c, pl.ds(b * SUB + 1, SUB), slice(None))],
                ref[(*lead, c, pl.ds(b * SUB - 1, SUB), slice(None))])

    def mask_state(b):
        at = block(b)
        for c in range(9):
            w = raw[4, c, at, :]
            pm[c, at, :] = w * pressure(raw[0, c, at, :], raw[1, c, at, :])
            for a in range(4):
                g[a, c, at, :] = w * raw[a, c, at, :]

    def constants(b):
        at = block(b)
        row = lat * rows + b * SUB - lo + row8
        row = jnp.where(row >= total, 2 * total - 1 - row, row).astype(jnp.float32)
        cor[at, :] = CORIOLIS_MAX * (2.0 * (row + 0.5) / total - 1.0)
        for c in range(9):
            w = raw[4, c, at, :]
            we, ww = columns(raw, (4,), c, at)
            wn, ws = lines(raw, (4,), c, b)
            s = (we + ww) + (wn + ws)
            tot[c, at, :] = s
            coef[c, at, :] = DIFFUSION + HYPERDIFF * s
            weak[c, at, :] = HYPERDIFF * w
            ax[c, at, :] = we - ww
            ay[c, at, :] = wn - ws

    def first_pass(b):
        at = block(b)
        f = cor[at, :]
        for c in range(9):
            w, s, k = raw[4, c, at, :], tot[c, at, :], coef[c, at, :]
            a_x, a_y = ax[c, at, :], ay[c, at, :]
            u, v = g[2, c, at, :], g[3, c, at, :]
            cu = (0.5 * ADVECTION) * u
            cv = (0.5 * ADVECTION) * v
            keep = 1.0 + (cu * a_x + cv * a_y)
            for a in range(4):
                x = g[a, c, at, :]
                xe, xw = columns(g, (a,), c, at)
                xn, xs = lines(g, (a,), c, b)
                lap = w * ((xe + xw) + (xn + xs)) - s * x
                lm[a, c, at, :] = lap
                new = keep * x - cu * (xe - xw) - cv * (xn - xs) + k * lap
                if a == 2:
                    pe, pw = columns(pm, (), c, at)
                    new = new + (f * v - w * (pe - pw) + a_x * pm[c, at, :])
                if a == 3:
                    pn, ps = lines(pm, (), c, b)
                    new = new - (f * u + w * (pn - ps) - a_y * pm[c, at, :])
                part[a, c, at, :] = new

    def second_pass(b, a, c):
        at = block(b)
        xe, xw = columns(lm, (a,), c, at)
        xn, xs = lines(lm, (a,), c, b)
        return part[a, c, at, :] - weak[c, at, :] * ((xe + xw) + (xn + xs))

    first_block = lo // SUB
    last_block = hi // SUB

    @pl.loop(first_block, last_block)
    def _(b):
        mask_state(b)

    @pl.loop(first_block + 1, last_block - 1)
    def _(b):
        constants(b)
        first_pass(b)

    @pl.when(is_north)
    def _():
        to_fold(main, 0).wait()
        to_fold(side, 3).wait()

    @pl.when(jnp.logical_not(is_north))
    def _():
        to_north(main, 1).wait_send()
        to_north(side, 4).wait_send()
        to_south(main, 2).wait_recv()
        to_south(side, 5).wait_recv()

    @pl.when(has_south)
    def _():
        to_south(main, 2).wait_send()
        to_south(side, 5).wait_send()
        to_north(main, 1).wait_recv()
        to_north(side, 4).wait_recv()

    mask_state(first_block - 1)
    mask_state(last_block)

    @pl.loop(0, 4)
    def _(k):
        b = jnp.where(k < 2, first_block - 1 + k, last_block - 3 + k)
        constants(b)
        first_pass(b)

    for step in range(STEPS):
        if step > 0:
            @pl.loop(first_block - 1, last_block + 1)
            def _(b):
                first_pass(b)

        if step < STEPS - 1:
            @pl.loop(first_block - 1, last_block + 1)
            def _(b):
                at = block(b)
                for c in range(9):
                    new = [second_pass(b, a, c) for a in range(4)]
                    pm[c, at, :] = raw[4, c, at, :] * pressure(new[0], new[1])
                    for a in range(4):
                        g[a, c, at, :] = new[a]
        else:
            @pl.loop(first_block, last_block)
            def _(b):
                at = pl.ds(pl.multiple_of((b - first_block) * SUB, SUB), SUB)
                for a in range(4):
                    regs = swap_bits([take(second_pass(b, a, c), to_cols) for c in range(8)], lane)
                    for l in range(8):
                        outs[a][l, at, :] = regs[l]


def shards(n_lon, n_lat, *fields):
    shape = fields[0].shape
    levels, rows, cols = shape
    assert levels == 8 and cols == LANES and rows % (2 * SUB) == 0 and rows >= 4 * SUB
    assert n_lon % 2 == 0 and n_lon > 2
    tall = rows + 4 * SUB
    vmem = pl.BlockSpec(memory_space=pltpu.VMEM)
    f32 = jnp.float32
    plane = pltpu.VMEM((9, tall, LANES), f32)
    state = pltpu.VMEM((4, 9, tall, LANES), f32)
    edge = pltpu.VMEM((5, rows // 2, LANES), f32)
    return tuple(pl.pallas_call(
        functools.partial(kernel, n_lon, n_lat, rows),
        out_shape=[jax.ShapeDtypeStruct(shape, f32)] * 4,
        in_specs=[vmem] * 5,
        out_specs=[vmem] * 4,
        scratch_shapes=[
            pltpu.VMEM((5, 9, tall, LANES), f32),
            state,
            plane,
            state,
            state,
            plane, plane, plane, plane, plane,
            pltpu.VMEM((tall, LANES), f32),
            pltpu.VMEM((5, 9, SUB, LANES), f32),
            edge, edge, edge, edge,
            pltpu.SemaphoreType.DMA((8,)),
            pltpu.SemaphoreType.DMA((8,)),
        ],
        compiler_params=pltpu.CompilerParams(
            collective_id=0, has_side_effects=True, vmem_limit_bytes=40 * 1024 * 1024),
    )(*fields))


def solution(mesh):
    placed = P(None, "lat", "lon")
    return jax.shard_map(
        functools.partial(shards, mesh.shape["lon"], mesh.shape["lat"]),
        mesh=mesh,
        in_specs=(placed,) * 5,
        out_specs=(placed,) * 4,
        check_vma=False,
    )
```

profile of v0, /device:TPU:3, one launch (start us, length us, event | category | flops | bytes accessed | tf_op | source)
XLA Modules:
  0.0 45.1 jit_solution(1878382637966292659)
XLA Ops:
  0.6 0.0 copy-start
  0.6 0.9 %copy-done = f32[8,64,128]{2,1,0:T(8,128)S(1)} copy-done((f32[8,64,128]{2,1,0:T(8,128)S(1)}, f32[8,64,128]{2,1,0:T(8,128)}, u32[]{:S(2)}) %copy-start) | copy-done | bytes 262168
  1.6 0.0 copy-start.1
  1.6 0.9 %copy-done.1 = f32[8,64,128]{2,1,0:T(8,128)S(1)} copy-done((f32[8,64,128]{2,1,0:T(8,128)S(1)}, f32[8,64,128]{2,1,0:T(8,128)}, u32[]{:S(2)}) %copy-start.1) | copy-done | bytes 262168
  2.5 0.0 copy-start.2
  2.5 0.9 %copy-done.2 = f32[8,64,128]{2,1,0:T(8,128)S(1)} copy-done((f32[8,64,128]{2,1,0:T(8,128)S(1)}, f32[8,64,128]{2,1,0:T(8,128)}, u32[]{:S(2)}) %copy-start.2) | copy-done | bytes 262168
  3.5 0.0 copy-start.3
  3.5 0.9 %copy-done.3 = f32[8,64,128]{2,1,0:T(8,128)S(1)} copy-done((f32[8,64,128]{2,1,0:T(8,128)S(1)}, f32[8,64,128]{2,1,0:T(8,128)}, u32[]{:S(2)}) %copy-start.3) | copy-done | bytes 262168
  4.4 0.0 copy-start.4
  4.4 0.9 %copy-done.4 = s32[8,64,128]{2,1,0:T(8,128)S(1)} copy-done((s32[8,64,128]{2,1,0:T(8,128)S(1)}, s32[8,64,128]{2,1,0:T(8,128)}, u32[]{:S(2)}) %copy-start.4) | copy-done | bytes 262168
  5.4 36.9 %shard_map.84 = (f32[8,64,128]{2,1,0:T(8,128)S(1)}, f32[8,64,128]{2,1,0:T(8,128)S(1)}, f32[8,64,128]{2,1,0:T(8,128)S(1)}, f32[8,64,128]{2,1,0:T(8,128)S(1)}) custom-call(f32[8,64,128]{2,1,0:T(8,128)S(1)} %copy-done, f32[8,64,128]{2,1,0:T(8,128)S(1)} %copy-done.1, f32[8,64,128]{2,1,0:T(8,128)S(1)} %copy-done.2, f32[8,64,128]{2,1,0:T(8,128)S(1)} %copy-done.3, ...), custom_call_target="tpu_custom_call" | custom-call | tf_op jit(solution)/shard_map/pallas_call | solution.py:365
  42.3 0.7 %copy.13 = f32[8,64,128]{2,1,0:T(8,128)} copy(f32[8,64,128]{2,1,0:T(8,128)S(1)} %get-tuple-element.8) | data formatting | bytes 524288
  43.0 0.7 %copy.14 = f32[8,64,128]{2,1,0:T(8,128)} copy(f32[8,64,128]{2,1,0:T(8,128)S(1)} %get-tuple-element.9) | data formatting | bytes 524288
  43.7 0.7 %copy.15 = f32[8,64,128]{2,1,0:T(8,128)} copy(f32[8,64,128]{2,1,0:T(8,128)S(1)} %get-tuple-element.10) | data formatting | bytes 524288
  44.4 0.7 %copy.16 = f32[8,64,128]{2,1,0:T(8,128)} copy(f32[8,64,128]{2,1,0:T(8,128)S(1)} %get-tuple-element.11) | data formatting | bytes 524288
Async XLA Ops:
  0.6 1.0 %copy-start = (f32[8,64,128]{2,1,0:T(8,128)S(1)}, f32[8,64,128]{2,1,0:T(8,128)}, u32[]{:S(2)}) copy-start(f32[8,64,128]{2,1,0:T(8,128)} %t_in.1) | copy-start | bytes 786436
  1.6 0.9 %copy-start.1 = (f32[8,64,128]{2,1,0:T(8,128)S(1)}, f32[8,64,128]{2,1,0:T(8,128)}, u32[]{:S(2)}) copy-start(f32[8,64,128]{2,1,0:T(8,128)} %s_in.1) | copy-start | bytes 786436
  2.5 0.9 %copy-start.2 = (f32[8,64,128]{2,1,0:T(8,128)S(1)}, f32[8,64,128]{2,1,0:T(8,128)}, u32[]{:S(2)}) copy-start(f32[8,64,128]{2,1,0:T(8,128)} %u_in.1) | copy-start | bytes 786436
  3.5 0.9 %copy-start.3 = (f32[8,64,128]{2,1,0:T(8,128)S(1)}, f32[8,64,128]{2,1,0:T(8,128)}, u32[]{:S(2)}) copy-start(f32[8,64,128]{2,1,0:T(8,128)} %v_in.1) | copy-start | bytes 786436
  4.4 0.9 %copy-start.4 = (s32[8,64,128]{2,1,0:T(8,128)S(1)}, s32[8,64,128]{2,1,0:T(8,128)}, u32[]{:S(2)}) copy-start(s32[8,64,128]{2,1,0:T(8,128)} %m_in.1) | copy-start | bytes 786436
where the time goes:
time: 45.4 us; the launch traced here: 45.1 us
  Pallas kernels  36.9 us (81%)
  local copies, waits for them, and re-layouts  7.55 us (17%)
  between operations  0.65 us (1%)
    pallas_call x1, Pallas kernels, shards(): pl.pallas_call(functools.partial(kernel, n_lon, n_lat, rows), out_shape=[...  36.9 us
    unnamed x14, local copies, waits for them, and re-layouts  7.55 us

commit v1 on v0

--- a/solution.py
+++ b/solution.py
@@ -34,7 +34,7 @@
 def swap_bits(regs, lane):
     regs = list(regs)
     for k in range(3):
-        dist = 16 << k
+        dist = 1 << k
         low = (lane & dist) == 0
         for a in range(8):
             if a & (1 << k):
@@ -46,9 +46,10 @@
     return regs
 
 
-def kernel(n_lon, n_lat, rows, t_in, s_in, u_in, v_in, m_in, t_out, s_out, u_out, v_out,
+def kernel(n_lon, n_lat, rows, t_hbm, s_hbm, u_hbm, v_hbm, m_hbm, t_out, s_out, u_out, v_out,
            raw, g, pm, lm, part, tot, coef, ax, ay, weak, cor,
-           fold, send_w, send_e, recv_w, recv_e, ssem, rsem):
+           fold, send_w, send_e, recv_w, recv_e, t_in, s_in, u_in, v_in, m_in,
+           ssem, rsem, isem):
     lo = 2 * SUB
     hi = lo + rows
     blocks = rows // SUB
@@ -64,6 +65,10 @@
     north_lon = jnp.where(is_north, mirror, lon)
     ins = (t_in, s_in, u_in, v_in, m_in)
     outs = (t_out, s_out, u_out, v_out)
+    loads = [pltpu.make_async_copy(src, dst, isem.at[k])
+             for k, (src, dst) in enumerate(zip((t_hbm, s_hbm, u_hbm, v_hbm, m_hbm), ins))]
+    for load in loads:
+        load.start()
 
     barrier = pltpu.get_barrier_semaphore()
     for target in ((west, lat), (east, lat), (north_lon, north_lat)):
@@ -74,8 +79,7 @@
         pl.semaphore_signal(barrier, inc=1, device_id=(lon, lat - 1), device_id_type=MESH)
 
     lane = lane_of((SUB, LANES))
-    to_flat = 16 * (lane & 7) + (lane >> 3)
-    to_cols = 8 * (lane & 15) + (lane >> 4)
+    rims = jnp.where(lane < 64, 0, LANES - 8) + (lane & 7)
     turned = 8 * (15 - (lane >> 3)) + (lane & 7)
     row8 = lax.broadcasted_iota(jnp.int32, (SUB, LANES), 0)
 
@@ -87,7 +91,11 @@
                 regs = [x.astype(jnp.float32) for x in regs]
             regs = swap_bits(regs, lane)
             for c in range(8):
-                raw[a, c, pl.ds(lo + r, SUB), :] = take(regs[c], to_flat)
+                raw[a, c, pl.ds(lo + r, SUB), :] = regs[c]
+            rim = take(regs[0], rims)
+            for c in range(1, 8):
+                rim = jnp.where(((lane >> 3) & 7) == c, take(regs[c], rims), rim)
+            raw[a, 8, pl.ds(lo + r, SUB), :] = rim
 
     def reverse_rows(x):
         for k in (4, 2, 1):
@@ -126,6 +134,8 @@
         return copy(raw.at[:, part_slice, lo:lo + SUB], raw.at[:, part_slice, hi:hi + SUB],
                     k, (lon, lat - 1))
 
+    for load in loads:
+        load.wait()
     bring(blocks - 1)
     bring(0)
 
@@ -170,11 +180,11 @@
 
     near = lane_of((half, LANES)) < 64
     for a in range(5):
-        first = raw[a, 0, lo:lo + half]
-        second = raw[a, 0, lo + half:hi]
+        first = raw[a, 8, lo:lo + half]
+        second = raw[a, 8, lo + half:hi]
         send_w[a] = jnp.where(near, first, pltpu.roll(second, 64, 1))
-        first = raw[a, 7, lo:lo + half]
-        second = raw[a, 7, lo + half:hi]
+        first = raw[a, 8, lo:lo + half]
+        second = raw[a, 8, lo + half:hi]
         send_e[a] = jnp.where(near, pltpu.roll(first, 64, 1), second)
     go_w = copy(send_w, recv_e, 6, (west, lat))
     go_e = copy(send_e, recv_w, 7, (east, lat))
@@ -221,11 +231,20 @@
         return pl.ds(pl.multiple_of(b * SUB, SUB), SUB)
 
     def columns(ref, lead, c, at):
-        x = ref[(*lead, c, at, slice(None))]
-        xe = ref[(*lead, (c + 1) % 9, at, slice(None))]
-        xw = ref[(*lead, (c + 8) % 9, at, slice(None))]
-        return (pltpu.roll(jnp.where(lane < 8, xe, x), LANES - 8, 1),
-                pltpu.roll(jnp.where(lane >= LANES - 8, xw, x), 8, 1))
+        def get(i):
+            return ref[(*lead, i, at, slice(None))]
+
+        if c < 7:
+            xe = get(c + 1)
+        else:
+            far, near_by = (8, 0) if c == 7 else (0, 8)
+            xe = pltpu.roll(jnp.where(lane < 8, get(far), get(near_by)), LANES - 8, 1)
+        if 0 < c < 8:
+            xw = get(c - 1)
+        else:
+            far, near_by = (8, 7) if c == 0 else (7, 8)
+            xw = pltpu.roll(jnp.where(lane >= LANES - 8, get(far), get(near_by)), 8, 1)
+        return xe, xw
 
     def lines(ref, lead, c, b):
         return (ref[(*lead, c, pl.ds(b * SUB + 1, SUB), slice(None))],
@@ -346,7 +365,7 @@
             def _(b):
                 at = pl.ds(pl.multiple_of((b - first_block) * SUB, SUB), SUB)
                 for a in range(4):
-                    regs = swap_bits([take(second_pass(b, a, c), to_cols) for c in range(8)], lane)
+                    regs = swap_bits([second_pass(b, a, c) for c in range(8)], lane)
                     for l in range(8):
                         outs[a][l, at, :] = regs[l]
 
@@ -362,10 +381,10 @@
     plane = pltpu.VMEM((9, tall, LANES), f32)
     state = pltpu.VMEM((4, 9, tall, LANES), f32)
     edge = pltpu.VMEM((5, rows // 2, LANES), f32)
-    return tuple(pl.pallas_call(
+    new = pl.pallas_call(
         functools.partial(kernel, n_lon, n_lat, rows),
         out_shape=[jax.ShapeDtypeStruct(shape, f32)] * 4,
-        in_specs=[vmem] * 5,
+        in_specs=[pl.BlockSpec(memory_space=pltpu.HBM)] * 5,
         out_specs=[vmem] * 4,
         scratch_shapes=[
             pltpu.VMEM((5, 9, tall, LANES), f32),
@@ -377,12 +396,16 @@
             pltpu.VMEM((tall, LANES), f32),
             pltpu.VMEM((5, 9, SUB, LANES), f32),
             edge, edge, edge, edge,
+            *[pltpu.VMEM(shape, x.dtype) for x in fields],
             pltpu.SemaphoreType.DMA((8,)),
             pltpu.SemaphoreType.DMA((8,)),
+            pltpu.SemaphoreType.DMA((5,)),
         ],
         compiler_params=pltpu.CompilerParams(
-            collective_id=0, has_side_effects=True, vmem_limit_bytes=40 * 1024 * 1024),
-    )(*fields))
+            collective_id=0, has_side_effects=True, vmem_limit_bytes=(64 * 1024 - 1024 - 128) * 1024),
+    )(*fields)
+    water = fields[4] != 0
+    return tuple(jnp.where(water, x, 0.0) for x in new)
 
 
 def solution(mesh):

time: 45.4 us -> 38 us (0.84)
  local copies, waits for them, and re-layouts: 7.55 us -> 0.02 us
  other arithmetic: 0 us -> 2.69 us
  Pallas kernels: 36.9 us -> 34.4 us
    unnamed x14 -> x8, local copies, waits for them, and re-layouts: 7.55 us -> 0.02 us
    select_n x0 -> x2, other arithmetic: none -> 2.69 us  [shards(): return tuple((jnp.where(water, x, 0.0) for x in new))]
    pallas_call x1, Pallas kernels: 36.9 us -> 34.4 us  [shards(): pl.pallas_call(functools.partial(kernel, n_lon, n_lat, rows), out_shape=[...]
where the time goes in v1:
time: 38 us; the launch traced here: 37.8 us
  Pallas kernels  34.4 us (91%)
  other arithmetic  2.69 us (7%)
  between operations  0.68 us (2%)
    pallas_call x1, Pallas kernels, shards(): pl.pallas_call(functools.partial(kernel, n_lon, n_lat, rows), out_shape=[...  34.4 us
    select_n x2, other arithmetic, shards(): return tuple((jnp.where(water, x, 0.0) for x in new))  2.69 us

profile of v1, /device:TPU:3, one launch (start us, length us, event | category | flops | bytes accessed | tf_op | source)
XLA Modules:
  0.0 37.8 jit_solution(13050010352561479935)
XLA Ops:
  0.6 0.0 copy-start
  0.6 34.4 %shard_map.84 = (f32[8,64,128]{2,1,0:T(8,128)}, f32[8,64,128]{2,1,0:T(8,128)}, f32[8,64,128]{2,1,0:T(8,128)}, f32[8,64,128]{2,1,0:T(8,128)}) custom-call(f32[8,64,128]{2,1,0:T(8,128)} %t_hbm.1, f32[8,64,128]{2,1,0:T(8,128)} %s_hbm.1, f32[8,64,128]{2,1,0:T(8,128)} %u_hbm.1, f32[8,64,128]{2,1,0:T(8,128)} %v_hbm.1, s32[8,64,128]{2,1,0:T(8,128)} %m_hbm.1), custom_call_target="tpu_custom_call" | custom-call | tf_op jit(solution)/shard_map/pallas_call | solution.py:384
  35.1 0.0 copy-done
  35.1 0.0 copy-start.1
  35.1 0.0 copy-start.2
  35.1 0.0 copy-start.3
  35.1 1.8 %broadcast_select_fusion = (f32[8,64,128]{2,1,0:T(8,128)}, pred[8,64,128]{2,1,0:T(8,128)(4,1)S(1)}) fusion(f32[8,64,128]{2,1,0:T(8,128)} %get-tuple-element.11, s32[8,64,128]{2,1,0:T(8,128)S(1)} %copy-done), kind=kLoop, calls=%fused_computation | loop fusion | flops 131072 | bytes 851968 | tf_op jit(solution)/shard_map/jit(_where)/select_n | solution.py:408
  36.9 0.0 copy-done.1
  36.9 0.0 copy-done.2
  36.9 0.0 copy-done.3
  36.9 0.9 %broadcast_select_fusion.1 = (f32[8,64,128]{2,1,0:T(8,128)}, f32[8,64,128]{2,1,0:T(8,128)}, f32[8,64,128]{2,1,0:T(8,128)}) fusion(pred[8,64,128]{2,1,0:T(8,128)(4,1)S(1)} %get-tuple-element.13, f32[8,64,128]{2,1,0:T(8,128)S(1)} %copy-done.3, f32[8,64,128]{2,1,0:T(8,128)S(1)} %copy-done.2, f32[8,64,128]{2,1,0:T(8,128)S(1)} %copy-done.1), kind=kLoop, calls=%fused_computation.1 | loop fusion | flops 196608 | bytes 1638400 | tf_op jit(solution)/shard_map/jit(_where)/select_n | solution.py:408
Async XLA Ops:
  0.6 34.4 %copy-start = (s32[8,64,128]{2,1,0:T(8,128)S(1)}, s32[8,64,128]{2,1,0:T(8,128)}, u32[]{:S(2)}) copy-start(s32[8,64,128]{2,1,0:T(8,128)} %m_hbm.1) | copy-start | bytes 786436
  35.1 1.8 %copy-start.1 = (f32[8,64,128]{2,1,0:T(8,128)S(1)}, f32[8,64,128]{2,1,0:T(8,128)}, u32[]{:S(2)}) copy-start(f32[8,64,128]{2,1,0:T(8,128)} %get-tuple-element.8) | copy-start | bytes 786436
  35.1 1.8 %copy-start.2 = (f32[8,64,128]{2,1,0:T(8,128)S(1)}, f32[8,64,128]{2,1,0:T(8,128)}, u32[]{:S(2)}) copy-start(f32[8,64,128]{2,1,0:T(8,128)} %get-tuple-element.9) | copy-start | bytes 786436
  35.1 1.8 %copy-start.3 = (f32[8,64,128]{2,1,0:T(8,128)S(1)}, f32[8,64,128]{2,1,0:T(8,128)}, u32[]{:S(2)}) copy-start(f32[8,64,128]{2,1,0:T(8,128)} %get-tuple-element.10) | copy-start | bytes 786436

commit v2 on v1

--- a/solution.py
+++ b/solution.py
@@ -204,19 +204,6 @@
         for a in range(5):
             raw[a, :, lo - SUB:lo, :] = nothing
 
-    go_w.wait()
-    go_e.wait()
-    for a in range(5):
-        x, y = recv_e[a], recv_w[a]
-        raw[a, 8, lo:lo + half] = jnp.where(near, x, pltpu.roll(y, 64, 1))
-        raw[a, 8, lo + half:hi] = jnp.where(near, pltpu.roll(x, 64, 1), y)
-
-    @pl.when(is_north)
-    def _():
-        fold_chunk(8, 8)
-
-    send_side()
-
     level = lane & 7
     scale = 0.5 * PRESSURE_COEF
     total = rows * n_lat
@@ -250,20 +237,20 @@
         return (ref[(*lead, c, pl.ds(b * SUB + 1, SUB), slice(None))],
                 ref[(*lead, c, pl.ds(b * SUB - 1, SUB), slice(None))])
 
-    def mask_state(b):
+    def mask_state(b, chunks=range(9)):
         at = block(b)
-        for c in range(9):
+        for c in chunks:
             w = raw[4, c, at, :]
             pm[c, at, :] = w * pressure(raw[0, c, at, :], raw[1, c, at, :])
             for a in range(4):
                 g[a, c, at, :] = w * raw[a, c, at, :]
 
-    def constants(b):
+    def constants(b, chunks=range(9)):
         at = block(b)
         row = lat * rows + b * SUB - lo + row8
         row = jnp.where(row >= total, 2 * total - 1 - row, row).astype(jnp.float32)
         cor[at, :] = CORIOLIS_MAX * (2.0 * (row + 0.5) / total - 1.0)
-        for c in range(9):
+        for c in chunks:
             w = raw[4, c, at, :]
             we, ww = columns(raw, (4,), c, at)
             wn, ws = lines(raw, (4,), c, b)
@@ -274,10 +261,10 @@
             ax[c, at, :] = we - ww
             ay[c, at, :] = wn - ws
 
-    def first_pass(b):
+    def first_pass(b, chunks=range(9)):
         at = block(b)
         f = cor[at, :]
-        for c in range(9):
+        for c in chunks:
             w, s, k = raw[4, c, at, :], tot[c, at, :], coef[c, at, :]
             a_x, a_y = ax[c, at, :], ay[c, at, :]
             u, v = g[2, c, at, :], g[3, c, at, :]
@@ -310,12 +297,34 @@
 
     @pl.loop(first_block, last_block)
     def _(b):
-        mask_state(b)
+        mask_state(b, range(8))
 
     @pl.loop(first_block + 1, last_block - 1)
     def _(b):
-        constants(b)
-        first_pass(b)
+        constants(b, range(1, 7))
+        first_pass(b, range(1, 7))
+
+    go_w.wait()
+    go_e.wait()
+    for a in range(5):
+        x, y = recv_e[a], recv_w[a]
+        raw[a, 8, lo:lo + half] = jnp.where(near, x, pltpu.roll(y, 64, 1))
+        raw[a, 8, lo + half:hi] = jnp.where(near, pltpu.roll(x, 64, 1), y)
+
+    @pl.when(is_north)
+    def _():
+        fold_chunk(8, 8)
+
+    send_side()
+
+    @pl.loop(first_block, last_block)
+    def _(b):
+        mask_state(b, (8,))
+
+    @pl.loop(first_block + 1, last_block - 1)
+    def _(b):
+        constants(b, (7, 8, 0))
+        first_pass(b, (7, 8, 0))
 
     @pl.when(is_north)
     def _():
@@ -347,12 +356,12 @@
 
     for step in range(STEPS):
         if step > 0:
-            @pl.loop(first_block - 1, last_block + 1)
+            @pl.loop(first_block - 1, last_block + 1, unroll=2)
             def _(b):
                 first_pass(b)
 
         if step < STEPS - 1:
-            @pl.loop(first_block - 1, last_block + 1)
+            @pl.loop(first_block - 1, last_block + 1, unroll=2)
             def _(b):
                 at = block(b)
                 for c in range(9):

time: 38 us -> 34.3 us (0.903)
  Pallas kernels: 34.4 us -> 30.8 us
    pallas_call x1, Pallas kernels: 34.4 us -> 30.8 us  [shards(): pl.pallas_call(functools.partial(kernel, n_lon, n_lat, rows), out_shape=[...]
where the time goes in v2:
time: 34.3 us; the launch traced here: 34.2 us
  Pallas kernels  30.8 us (90%)
  other arithmetic  2.69 us (8%)
  between operations  0.68 us (2%)
    pallas_call x1, Pallas kernels, shards(): pl.pallas_call(functools.partial(kernel, n_lon, n_lat, rows), out_shape=[...  30.8 us
    select_n x2, other arithmetic, shards(): return tuple((jnp.where(water, x, 0.0) for x in new))  2.69 us

profile of v2, /device:TPU:3, one launch (start us, length us, event | category | flops | bytes accessed | tf_op | source)
XLA Modules:
  0.0 34.2 jit_solution(1092820982307837829)
XLA Ops:
  0.6 0.0 copy-start
  0.6 30.8 %shard_map.84 = (f32[8,64,128]{2,1,0:T(8,128)}, f32[8,64,128]{2,1,0:T(8,128)}, f32[8,64,128]{2,1,0:T(8,128)}, f32[8,64,128]{2,1,0:T(8,128)}) custom-call(f32[8,64,128]{2,1,0:T(8,128)} %t_hbm.1, f32[8,64,128]{2,1,0:T(8,128)} %s_hbm.1, f32[8,64,128]{2,1,0:T(8,128)} %u_hbm.1, f32[8,64,128]{2,1,0:T(8,128)} %v_hbm.1, s32[8,64,128]{2,1,0:T(8,128)} %m_hbm.1), custom_call_target="tpu_custom_call" | custom-call | tf_op jit(solution)/shard_map/pallas_call | solution.py:393
  31.4 0.0 copy-done
  31.4 0.0 copy-start.1
  31.4 0.0 copy-start.2
  31.5 0.0 copy-start.3
  31.5 1.8 %broadcast_select_fusion = (f32[8,64,128]{2,1,0:T(8,128)}, pred[8,64,128]{2,1,0:T(8,128)(4,1)S(1)}) fusion(f32[8,64,128]{2,1,0:T(8,128)} %get-tuple-element.11, s32[8,64,128]{2,1,0:T(8,128)S(1)} %copy-done), kind=kLoop, calls=%fused_computation | loop fusion | flops 131072 | bytes 851968 | tf_op jit(solution)/shard_map/jit(_where)/select_n | solution.py:417
  33.2 0.0 copy-done.1
  33.2 0.0 copy-done.2
  33.2 0.0 copy-done.3
  33.2 0.9 %broadcast_select_fusion.1 = (f32[8,64,128]{2,1,0:T(8,128)}, f32[8,64,128]{2,1,0:T(8,128)}, f32[8,64,128]{2,1,0:T(8,128)}) fusion(pred[8,64,128]{2,1,0:T(8,128)(4,1)S(1)} %get-tuple-element.13, f32[8,64,128]{2,1,0:T(8,128)S(1)} %copy-done.3, f32[8,64,128]{2,1,0:T(8,128)S(1)} %copy-done.2, f32[8,64,128]{2,1,0:T(8,128)S(1)} %copy-done.1), kind=kLoop, calls=%fused_computation.1 | loop fusion | flops 196608 | bytes 1638400 | tf_op jit(solution)/shard_map/jit(_where)/select_n | solution.py:417
Async XLA Ops:
  0.6 30.8 %copy-start = (s32[8,64,128]{2,1,0:T(8,128)S(1)}, s32[8,64,128]{2,1,0:T(8,128)}, u32[]{:S(2)}) copy-start(s32[8,64,128]{2,1,0:T(8,128)} %m_hbm.1) | copy-start | bytes 786436
  31.4 1.8 %copy-start.1 = (f32[8,64,128]{2,1,0:T(8,128)S(1)}, f32[8,64,128]{2,1,0:T(8,128)}, u32[]{:S(2)}) copy-start(f32[8,64,128]{2,1,0:T(8,128)} %get-tuple-element.8) | copy-start | bytes 786436
  31.4 1.8 %copy-start.2 = (f32[8,64,128]{2,1,0:T(8,128)S(1)}, f32[8,64,128]{2,1,0:T(8,128)}, u32[]{:S(2)}) copy-start(f32[8,64,128]{2,1,0:T(8,128)} %get-tuple-element.9) | copy-start | bytes 786436
  31.5 1.8 %copy-start.3 = (f32[8,64,128]{2,1,0:T(8,128)S(1)}, f32[8,64,128]{2,1,0:T(8,128)}, u32[]{:S(2)}) copy-start(f32[8,64,128]{2,1,0:T(8,128)} %get-tuple-element.10) | copy-start | bytes 786436
